TPU v7x, 32 devices: a whole 2x2x4 slice. The times are simulated.
32 devices in a mesh: uly: 4 (over y, x), blk: 8 (over z, core).
Axes of the slice: x: 2, y: 2, z: 4, core: 2. Of those that a mesh axis runs over, the one named last changes fastest.
Arguments:
- queries: bfloat16 [2048, 2048], P(('uly', 'blk')), may hold values from -6 to 6
- key_vector_rows: bfloat16 [2048, 256], P(('uly', 'blk')), may hold values from -6 to 6
- value_vector_rows: bfloat16 [2048, 256], P(('uly', 'blk')), may hold values from -6 to 6
- out_grad: bfloat16 [2048, 2048], P(('uly', 'blk')), may hold values from -6 to 6
- block_list: int32 [16, 16, 8], P('uly'), may hold values from 0 to 15, as said below
Outputs:
- attended: bfloat16 [2048, 2048], P(('uly', 'blk'))
- query_grad: bfloat16 [2048, 2048], P(('uly', 'blk'))
- gradient_keys: bfloat16 [2048, 256], P(('uly', 'blk'))
- gradient_values: bfloat16 [2048, 256], P(('uly', 'blk'))
Inputs may be any that keep to these rules, and one draw needn't show every extreme that they name: block_list[h, i] names key blocks for query block i of head h: its first entry is always i itself, every entry is at most i, and a block may be named several times.
All inputs are finite; a program needn't handle non-finite values.
Results may differ from a plain program's by a relative error of at most 0.039.
Values may be sent and summed in bfloat16 or wider, within the bound.
A program may use at most 128 MiB of HBM per device.

v0:
```python
import math

import jax
import jax.numpy as jnp
from jax import lax
from jax.sharding import PartitionSpec as P

KEY_VALUE_HEADS = 2
HEAD_SIZE = 128
BLOCK = 128


def body(queries, key_vector_rows, value_vector_rows, out_grad, block_list):
    ulysses_width = lax.axis_size("uly")
    cycle_size = lax.axis_size("blk")
    segment_length = queries.shape[0]
    heads_dev = block_list.shape[0]
    list_len = block_list.shape[2]
    head_width = heads_dev * HEAD_SIZE
    copy_count = ulysses_width // KEY_VALUE_HEADS
    cycle_index = lax.axis_index("blk")
    score_scale = 1.0 / math.sqrt(HEAD_SIZE)
    sub_length = min(segment_length, BLOCK)
    sub_count = segment_length // sub_length
    unit_len = min(segment_length, BLOCK)
    units_per_block = BLOCK // unit_len
    units_per_segment = segment_length // unit_len
    total_tokens = segment_length * ulysses_width * cycle_size
    units_total = total_tokens // unit_len
    query_slots = queries.reshape(segment_length, ulysses_width, head_width)
    grad_slots = out_grad.reshape(segment_length, ulysses_width, head_width)
    kv_local = jnp.concatenate(
        [
            key_vector_rows.reshape(segment_length, KEY_VALUE_HEADS, HEAD_SIZE),
            value_vector_rows.reshape(segment_length, KEY_VALUE_HEADS, HEAD_SIZE),
        ],
        axis=2,
    )
    kv_slots = jnp.repeat(kv_local, copy_count, axis=1)
    query_all, kv_mine, grad_all = (
        lax.all_to_all(query_slots, "uly", split_axis=1, concat_axis=0, tiled=True),
        lax.all_to_all(kv_slots, "uly", split_axis=1, concat_axis=0, tiled=True),
        lax.all_to_all(grad_slots, "uly", split_axis=1, concat_axis=0, tiled=True),
    )
    keys_all = lax.all_gather(kv_mine[:, 0, :], "blk", axis=0, tiled=True)
    item_count = heads_dev * ulysses_width * sub_count
    query_items = (
        query_all.reshape(ulysses_width, sub_count, sub_length, heads_dev, HEAD_SIZE)
        .transpose(3, 0, 1, 2, 4)
        .reshape(item_count, sub_length, HEAD_SIZE)
    )
    grad_items = (
        grad_all.reshape(ulysses_width, sub_count, sub_length, heads_dev, HEAD_SIZE)
        .transpose(3, 0, 1, 2, 4)
        .reshape(item_count, sub_length, HEAD_SIZE)
    )
    item_ids = jnp.arange(item_count, dtype=jnp.int32)
    head_ids = item_ids // (ulysses_width * sub_count)
    slot_ids = item_ids // sub_count % ulysses_width
    sub_ids = item_ids % sub_count
    segments = slot_ids * cycle_size + cycle_index
    first_pos = segments * segment_length + sub_ids * sub_length
    query_block = first_pos // BLOCK
    entries = block_list[head_ids, query_block]
    earlier = jnp.arange(list_len)[:, None] > jnp.arange(list_len)[None, :]
    repeated = jnp.any((entries[:, :, None] == entries[:, None, :]) & earlier[None, :, :], axis=2)
    offsets = jnp.arange(BLOCK, dtype=jnp.int32)
    key_pos = (entries[:, :, None] * BLOCK + offsets[None, None, :]).reshape(
        item_count, list_len * BLOCK
    )
    live_keys = jnp.repeat(jnp.logical_not(repeated), BLOCK, axis=1)
    query_pos = first_pos[:, None] + jnp.arange(sub_length, dtype=jnp.int32)[None, :]
    allowed = (key_pos[:, None, :] <= query_pos[:, :, None]) & live_keys[:, None, :]
    unit_count = list_len * units_per_block
    natural_units = (
        entries[:, :, None] * units_per_block
        + jnp.arange(units_per_block, dtype=jnp.int32)[None, None, :]
    ).reshape(item_count, unit_count)
    unit_seg = natural_units // units_per_segment
    canon_units = (
        unit_seg % cycle_size * ulysses_width + unit_seg // cycle_size
    ) * units_per_segment + natural_units % units_per_segment
    keys_units = keys_all.reshape(units_total, unit_len * 2 * HEAD_SIZE)
    unit_iota = jnp.arange(units_total, dtype=jnp.int32)
    per_step = min(item_count, max(1, 512 // sub_length))
    step_count = item_count // per_step
    key_len = list_len * BLOCK

    def group_step(grad_acc, group_data):
        query_group, grad_group, fetch_group, canon_group, mask_group = group_data
        fetch_table = (fetch_group.reshape(-1)[:, None] == unit_iota[None, :]).astype(jnp.bfloat16)
        gathered = (
            jnp.dot(fetch_table, keys_units, preferred_element_type=jnp.float32)
            .astype(jnp.bfloat16)
            .reshape(per_step, key_len, 2 * HEAD_SIZE)
        )
        key_group = gathered[:, :, :HEAD_SIZE]
        value_group = gathered[:, :, HEAD_SIZE:]
        scores = (
            jnp.einsum("nqd,nkd->nqk", query_group, key_group, preferred_element_type=jnp.float32)
            * score_scale
        )
        masked = jnp.where(mask_group, scores, -1e30)
        row_max = jnp.max(masked, axis=2, keepdims=True)
        row_sum = jnp.sum(
            jnp.where(mask_group, jnp.exp(masked - row_max), 0.0), axis=2, keepdims=True
        )
        log_sum = row_max + jnp.log(row_sum)
        weights = jnp.where(mask_group, jnp.exp(masked - log_sum), 0.0)
        weights_low = weights.astype(jnp.bfloat16)
        out_group = jnp.einsum(
            "nqk,nkd->nqd", weights_low, value_group, preferred_element_type=jnp.float32
        ).astype(jnp.bfloat16)
        row_dot = jnp.sum(
            grad_group.astype(jnp.float32) * out_group.astype(jnp.float32), axis=2, keepdims=True
        )
        grad_weights = jnp.einsum(
            "nqd,nkd->nqk", grad_group, value_group, preferred_element_type=jnp.float32
        )
        score_grad = (weights * (grad_weights - row_dot) * score_scale).astype(jnp.bfloat16)
        query_group_grad = jnp.einsum(
            "nqk,nkd->nqd", score_grad, key_group, preferred_element_type=jnp.float32
        ).astype(jnp.bfloat16)
        key_portion = jnp.einsum(
            "nqk,nqd->nkd", score_grad, query_group, preferred_element_type=jnp.float32
        )
        value_portion = jnp.einsum(
            "nqk,nqd->nkd", weights_low, grad_group, preferred_element_type=jnp.float32
        )
        both_parts = jnp.concatenate([key_portion, value_portion], axis=2).reshape(
            per_step * unit_count, unit_len * 2 * HEAD_SIZE
        )
        place_table = (canon_group.reshape(-1)[:, None] == unit_iota[None, :]).astype(jnp.float32)
        grad_acc = grad_acc + jnp.dot(
            place_table.T,
            both_parts,
            preferred_element_type=jnp.float32,
            precision=lax.Precision.HIGHEST,
        )
        return (grad_acc, (out_group, query_group_grad))

    empty_grad = jnp.zeros((units_total, unit_len * 2 * HEAD_SIZE), jnp.float32)
    scan_inputs = (
        query_items.reshape(step_count, per_step, sub_length, HEAD_SIZE),
        grad_items.reshape(step_count, per_step, sub_length, HEAD_SIZE),
        canon_units.reshape(step_count, per_step, unit_count),
        canon_units.reshape(step_count, per_step, unit_count),
        allowed.reshape(step_count, per_step, sub_length, key_len),
    )
    unit_grads, item_outputs = lax.scan(group_step, empty_grad, scan_inputs)
    kv_grad_all = unit_grads.reshape(total_tokens, 2 * HEAD_SIZE)
    out_items = (
        item_outputs[0]
        .reshape(heads_dev, ulysses_width, sub_count, sub_length, HEAD_SIZE)
        .transpose(1, 2, 3, 0, 4)
        .reshape(ulysses_width * segment_length, 1, head_width)
    )
    qgrad_items = (
        item_outputs[1]
        .reshape(heads_dev, ulysses_width, sub_count, sub_length, HEAD_SIZE)
        .transpose(1, 2, 3, 0, 4)
        .reshape(ulysses_width * segment_length, 1, head_width)
    )
    attended_back, qgrad_back = (
        lax.all_to_all(out_items, "uly", split_axis=0, concat_axis=1, tiled=True),
        lax.all_to_all(qgrad_items, "uly", split_axis=0, concat_axis=1, tiled=True),
    )
    attended = attended_back.reshape(segment_length, ulysses_width * head_width)
    query_grad = qgrad_back.reshape(segment_length, ulysses_width * head_width)
    owned = lax.psum_scatter(kv_grad_all, "blk", scatter_dimension=0, tiled=True)
    result_tuple = lax.all_to_all(
        owned.reshape(ulysses_width * segment_length, 1, 2 * HEAD_SIZE),
        "uly",
        split_axis=0,
        concat_axis=1,
        tiled=True,
    )
    summed_total = result_tuple.reshape(
        segment_length, KEY_VALUE_HEADS, copy_count, 2 * HEAD_SIZE
    ).sum(axis=2)
    gradient_keys = (
        summed_total[:, :, :HEAD_SIZE]
        .reshape(segment_length, KEY_VALUE_HEADS * HEAD_SIZE)
        .astype(jnp.bfloat16)
    )
    gradient_values = (
        summed_total[:, :, HEAD_SIZE:]
        .reshape(segment_length, KEY_VALUE_HEADS * HEAD_SIZE)
        .astype(jnp.bfloat16)
    )
    return (attended, query_grad, gradient_keys, gradient_values)


def solution(mesh):
    in_specs = (
        P(("uly", "blk"), None),
        P(("uly", "blk"), None),
        P(("uly", "blk"), None),
        P(("uly", "blk"), None),
        P("uly", None, None),
    )
    out_specs = (
        P(("uly", "blk"), None),
        P(("uly", "blk"), None),
        P(("uly", "blk"), None),
        P(("uly", "blk"), None),
    )
    return jax.shard_map(body, mesh=mesh, in_specs=in_specs, out_specs=out_specs, check_vma=False)
```

profile of v0, /device:TPU:0, one launch (start us, length us, event | category | flops | bytes accessed | tf_op | source)
XLA Modules:
  0.0 204.1 jit_solution(3762303482578430519)
XLA Ops:
  9.5 5.2 %all-to-all-start.1 = ((bf16[64,4,256]{2,0,1:T(8,128)(2,1)}), bf16[64,4,256]{2,0,1:T(8,128)(2,1)S(1)}, u32[]{:S(2)}, u32[]{:S(2)}) async-start(bf16[64,4,256]{2,0,1:T(8,128)(2,1)} %bitcast.6), calls=%async_computation.1 | async-start | bytes 262144 | tf_op jit(solution)/shard_map/all_to_all | solution.py:42
  16.4 3.3 %all-to-all-done.1 = bf16[64,4,256]{2,0,1:T(8,128)(2,1)S(1)} async-done(((bf16[64,4,256]{2,0,1:T(8,128)(2,1)}), bf16[64,4,256]{2,0,1:T(8,128)(2,1)S(1)}, u32[]{:S(2)}, u32[]{:S(2)}) %all-to-all-start.1) | async-done | bytes 131104 | tf_op jit(solution)/shard_map/all_to_all | solution.py:42
  19.7 3.4 %all-to-all-start = ((bf16[64,4,512]{2,0,1:T(8,128)(2,1)}), bf16[64,4,512]{2,0,1:T(8,128)(2,1)S(1)}, u32[]{:S(2)}, u32[]{:S(2)}) async-start(bf16[64,4,512]{2,0,1:T(8,128)(2,1)} %bitcast.109), calls=%async_computation | async-start | bytes 524288 | tf_op jit(solution)/shard_map/all_to_all | solution.py:41
  28.5 4.0 %all-to-all-start.2 = ((bf16[64,4,512]{2,0,1:T(8,128)(2,1)}), bf16[64,4,512]{2,0,1:T(8,128)(2,1)}, u32[]{:S(2)}, u32[]{:S(2)}) async-start(bf16[64,4,512]{2,0,1:T(8,128)(2,1)} %bitcast.108), calls=%async_computation.2 | async-start | bytes 524288 | tf_op jit(solution)/shard_map/all_to_all | solution.py:43
  35.3 2.7 %all-to-all-done.2 = bf16[64,4,512]{2,0,1:T(8,128)(2,1)} async-done(((bf16[64,4,512]{2,0,1:T(8,128)(2,1)}), bf16[64,4,512]{2,0,1:T(8,128)(2,1)}, u32[]{:S(2)}, u32[]{:S(2)}) %all-to-all-start.2) | async-done | bytes 262176 | tf_op jit(solution)/shard_map/all_to_all | solution.py:43
  37.9 1.7 reshape.303
  39.7 1.7 copy.95
  41.4 8.0 %all-gather.2.cloned.1.call-done = bf16[2048,256]{1,0:T(8,128)(2,1)} async-done(((bf16[256,256]{1,0:T(8,128)(2,1)}), bf16[2048,256]{1,0:T(8,128)(2,1)}) %all-gather.2.cloned.1.call-update) | async-done | bytes 1048592 | tf_op jit(solution)/shard_map/all_gather | solution.py:45
  49.4 2.3 %reshape.301 = bf16[32,16384]{1,0:T(8,128)(2,1)} reshape(bf16[2048,256]{1,0:T(8,128)(2,1)} %all-gather.2.cloned.1.call-done) | data formatting | bytes 2097152 | tf_op jit(solution)/shard_map/reshape | solution.py:83
  51.7 96.9 %while.16 = (s32[]{:T(128)}, f32[32,16384]{1,0:T(8,128)S(1)}, bf16[2,8,64,128]{3,2,1,0:T(8,128)(2,1)}, bf16[2,8,64,128]{3,2,1,0:T(8,128)(2,1)}, s32[2,8,16]{2,1,...) while((s32[]{:T(128)}, f32[32,16384]{1,0:T(8,128)S(1)}, ...), condition=%wide.region_5.6_spmd.clone, body=%wide.region_1.5_spmd.clone.sunk | while | flops 1759910912 | bytes 130718968 | solution.py:150
  51.8 4.5 %convolution_convert_fusion.2 = bf16[128,16384]{1,0:T(8,128)(2,1)} fusion(bf16[32,16384]{1,0:T(8,128)(2,1)} %get-tuple-element.291, s32[128]{0:T(128)S(1)} %eq.82), kind=kOutput, calls=%fused_computation.2.clone.1 | convolution fusion | flops 136318976 | bytes 5243392 | tf_op jit(solution)/shard_map/while/body/eval_jaxpr/dot_general | solution.py:93
  56.2 7.4 %reshape.329 = bf16[8,1024,256]{2,1,0:T(8,128)(2,1)} reshape(bf16[128,16384]{1,0:T(8,128)(2,1)} %convolution_convert_fusion.2) | data formatting | bytes 8388608 | tf_op jit(solution)/shard_map/while/body/eval_jaxpr/reshape | solution.py:95
  63.7 2.7 %fusion.88 = (f32[8,64]{1,0:T(8,128)S(1)}, f32[8,64,1024]{2,1,0:T(8,128)S(1)}) fusion(bf16[8,1024,256]{2,1,0:T(8,128)(2,1)} %reshape.329, bf16[2,8,64,128]{3,2,1,0:T(8,128)(2,1)S(1)} %get-tuple-element.290, s32[]{:T(128)S(6)} %copy.132, pred[2,8,64,1024]{3,2,1,0:T(32,128)(4,1)S(1)} %get-tuple-element.289), kind=kOutput, calls=%fused_computation.92.clone.1 | convolution fusion | flops 135790080 | bytes 4852736 | tf_op jit(solution)/shard_map/while/body/eval_jaxpr/nqd,nkd->nqk/dot_general | solution.py:100
  71.9 4.1 %pad_maximum_fusion.3 = f32[8,1024,256]{1,2,0:T(8,128)} fusion(f32[8,1024,128]{1,2,0:T(8,128)S(1)} %fusion.89, f32[8,1024,128]{1,2,0:T(8,128)S(1)} %fusion.90), kind=kLoop, calls=%fused_computation.4.clone.1 | loop fusion | flops 2097152 | bytes 16777216 | tf_op jit(solution)/shard_map/while/body/eval_jaxpr/concatenate | solution.py:130
  76.0 9.2 %copy.125 = f32[8,1024,256]{2,1,0:T(8,128)} copy(f32[8,1024,256]{1,2,0:T(8,128)} %pad_maximum_fusion.3) | data formatting | bytes 16777216 | tf_op jit(solution)/shard_map/while/body/eval_jaxpr/concatenate | solution.py:130
  85.1 9.4 %reshape.330 = f32[128,16384]{1,0:T(8,128)} reshape(f32[8,1024,256]{2,1,0:T(8,128)} %copy.125) | data formatting | bytes 16777216 | tf_op jit(solution)/shard_map/while/body/eval_jaxpr/reshape | solution.py:130
  94.5 5.6 %convolution_add_fusion.2 = f32[32,16384]{1,0:T(8,128)S(1)} fusion(f32[128,16384]{1,0:T(8,128)} %reshape.330, f32[32,16384]{1,0:T(8,128)S(1)} %get-tuple-element.274, pred[]{:T(512)S(6)} %compare.31, s32[128]{0:T(128)S(1)} %eq.82), kind=kOutput, calls=%fused_computation.3.clone.1 | convolution fusion | flops 806359040 | bytes 12583425 | tf_op jit(solution)/shard_map/while/body/eval_jaxpr/dot_general | solution.py:134
  100.2 4.5 %convolution_convert_fusion.2 = bf16[128,16384]{1,0:T(8,128)(2,1)} fusion(bf16[32,16384]{1,0:T(8,128)(2,1)} %get-tuple-element.291, s32[128]{0:T(128)S(1)} %eq.82), kind=kOutput, calls=%fused_computation.2.clone.1 | convolution fusion | flops 136318976 | bytes 5243392 | tf_op jit(solution)/shard_map/while/body/eval_jaxpr/dot_general | solution.py:93
  104.7 7.4 %reshape.329 = bf16[8,1024,256]{2,1,0:T(8,128)(2,1)} reshape(bf16[128,16384]{1,0:T(8,128)(2,1)} %convolution_convert_fusion.2) | data formatting | bytes 8388608 | tf_op jit(solution)/shard_map/while/body/eval_jaxpr/reshape | solution.py:95
  112.1 2.7 %fusion.88 = (f32[8,64]{1,0:T(8,128)S(1)}, f32[8,64,1024]{2,1,0:T(8,128)S(1)}) fusion(bf16[8,1024,256]{2,1,0:T(8,128)(2,1)} %reshape.329, bf16[2,8,64,128]{3,2,1,0:T(8,128)(2,1)S(1)} %get-tuple-element.290, s32[]{:T(128)S(6)} %copy.132, pred[2,8,64,1024]{3,2,1,0:T(32,128)(4,1)S(1)} %get-tuple-element.289), kind=kOutput, calls=%fused_computation.92.clone.1 | convolution fusion | flops 135790080 | bytes 4852736 | tf_op jit(solution)/shard_map/while/body/eval_jaxpr/nqd,nkd->nqk/dot_general | solution.py:100
  120.3 4.1 %pad_maximum_fusion.3 = f32[8,1024,256]{1,2,0:T(8,128)} fusion(f32[8,1024,128]{1,2,0:T(8,128)S(1)} %fusion.89, f32[8,1024,128]{1,2,0:T(8,128)S(1)} %fusion.90), kind=kLoop, calls=%fused_computation.4.clone.1 | loop fusion | flops 2097152 | bytes 16777216 | tf_op jit(solution)/shard_map/while/body/eval_jaxpr/concatenate | solution.py:130
  124.4 9.2 %copy.125 = f32[8,1024,256]{2,1,0:T(8,128)} copy(f32[8,1024,256]{1,2,0:T(8,128)} %pad_maximum_fusion.3) | data formatting | bytes 16777216 | tf_op jit(solution)/shard_map/while/body/eval_jaxpr/concatenate | solution.py:130
  133.6 9.4 %reshape.330 = f32[128,16384]{1,0:T(8,128)} reshape(f32[8,1024,256]{2,1,0:T(8,128)} %copy.125) | data formatting | bytes 16777216 | tf_op jit(solution)/shard_map/while/body/eval_jaxpr/reshape | solution.py:130
  142.9 5.6 %convolution_add_fusion.2 = f32[32,16384]{1,0:T(8,128)S(1)} fusion(f32[128,16384]{1,0:T(8,128)} %reshape.330, f32[32,16384]{1,0:T(8,128)S(1)} %get-tuple-element.274, pred[]{:T(512)S(6)} %compare.31, s32[128]{0:T(128)S(1)} %eq.82), kind=kOutput, calls=%fused_computation.3.clone.1 | convolution fusion | flops 806359040 | bytes 12583425 | tf_op jit(solution)/shard_map/while/body/eval_jaxpr/dot_general | solution.py:134
  151.9 2.2 %reduce.1 = bf16[256,512]{1,0:T(8,128)(2,1)S(1)} reduce(bf16[256,1,512]{2,1,0:T(2,128)(2,1)S(1)} %reshape.322, bf16[]{:T(256)} %broadcast.435), dimensions={1}, to_apply=%reshape.322.reduce_sub_computation | reduce | bytes 524290 | tf_op jit(solution)/shard_map/reshape | solution.py:162
  155.0 3.6 %all-to-all-start.4 = ((bf16[4,2,16384]{2,1,0:T(2,128)(2,1)}), bf16[4,2,16384]{2,1,0:T(2,128)(2,1)S(1)}, u32[]{:S(2)}, u32[]{:S(2)}) async-start(bf16[4,2,16384]{2,1,0:T(2,128)(2,1)} %reshape.325), calls=%async_computation.4 | async-start | bytes 524288 | tf_op jit(solution)/shard_map/all_to_all | solution.py:166
  160.0 2.2 %reduce = bf16[256,512]{1,0:T(8,128)(2,1)S(1)} reduce(bf16[256,1,512]{2,1,0:T(2,128)(2,1)S(1)} %reshape.321, bf16[]{:T(256)} %broadcast.435), dimensions={1}, to_apply=%reshape.321.reduce_sub_computation | reduce | bytes 524290 | tf_op jit(solution)/shard_map/reshape | solution.py:156
  164.4 3.4 %all-to-all-start.3 = ((bf16[4,2,16384]{2,1,0:T(2,128)(2,1)}), bf16[4,2,16384]{2,1,0:T(2,128)(2,1)S(1)}, u32[]{:S(2)}, u32[]{:S(2)}) async-start(bf16[4,2,16384]{2,1,0:T(2,128)(2,1)} %reshape.323), calls=%async_computation.3 | async-start | bytes 524288 | tf_op jit(solution)/shard_map/all_to_all | solution.py:165
  167.9 17.8 %reduce-scatter.2.cloned.1.call-done = f32[256,256]{1,0:T(8,128)} async-done(((f32[2048,256]{1,0:T(8,128)}), f32[256,256]{1,0:T(8,128)}) %reduce-scatter.2.cloned.1.call-update) | async-done | bytes 262160 | tf_op jit(solution)/shard_map/reduce_scatter | solution.py:170
  185.7 1.8 reshape.311
  187.5 3.7 %all-to-all-start.5 = ((f32[256,1,256]{2,1,0:T(1,128)}), f32[256,1,256]{2,1,0:T(1,128)S(1)}, u32[]{:S(2)}, u32[]{:S(2)}) async-start(f32[256,1,256]{2,1,0:T(1,128)} %reshape.311), calls=%async_computation.6 | async-start | bytes 524288 | tf_op jit(solution)/shard_map/all_to_all | solution.py:171
  193.8 2.8 %all-to-all-done.5 = f32[256,1,256]{2,1,0:T(1,128)S(1)} async-done(((f32[256,1,256]{2,1,0:T(1,128)}), f32[256,1,256]{2,1,0:T(1,128)S(1)}, u32[]{:S(2)}, u32[]{:S(2)}) %all-to-all-start.5) | async-done | bytes 262176 | tf_op jit(solution)/shard_map/all_to_all | solution.py:171
  (106 shorter events, 34.0 us)
Async XLA Ops:
  7.2 19.1 %copy-start.3 = (bf16[64,2048]{1,0:T(8,128)(2,1)S(1)}, bf16[64,2048]{1,0:T(8,128)(2,1)}, u32[]{:S(2)}) copy-start(bf16[64,2048]{1,0:T(8,128)(2,1)} %param.10) | copy-start | bytes 786436
  9.5 10.2 %all-to-all-start.1 = ((bf16[64,4,256]{2,0,1:T(8,128)(2,1)}), bf16[64,4,256]{2,0,1:T(8,128)(2,1)S(1)}, u32[]{:S(2)}, u32[]{:S(2)}) async-start(bf16[64,4,256]{2,0,1:T(8,128)(2,1)} %bitcast.6), calls=%async_computation.1 | async-start | bytes 262144 | tf_op jit(solution)/shard_map/all_to_all | solution.py:42
  19.7 3.5 %copy-start.2 = (bf16[64,4,256]{2,0,1:T(8,128)(2,1)}, bf16[64,4,256]{2,0,1:T(8,128)(2,1)S(1)}, u32[]{:S(2)}) copy-start(bf16[64,4,256]{2,0,1:T(8,128)(2,1)S(1)} %all-to-all-done.1) | copy-start | bytes 393220
  19.7 8.8 %all-to-all-start = ((bf16[64,4,512]{2,0,1:T(8,128)(2,1)}), bf16[64,4,512]{2,0,1:T(8,128)(2,1)S(1)}, u32[]{:S(2)}, u32[]{:S(2)}) async-start(bf16[64,4,512]{2,0,1:T(8,128)(2,1)} %bitcast.109), calls=%async_computation | async-start | bytes 524288 | tf_op jit(solution)/shard_map/all_to_all | solution.py:41
  23.1 26.2 %all-gather.2.cloned.1.call-start = ((), (), s32[]{:S(2)}) async-start(), calls=%async_computation.7 | async-start | bytes 1179648 | tf_op jit(solution)/shard_map/all_gather | solution.py:45
  28.5 9.5 %all-to-all-start.2 = ((bf16[64,4,512]{2,0,1:T(8,128)(2,1)}), bf16[64,4,512]{2,0,1:T(8,128)(2,1)}, u32[]{:S(2)}, u32[]{:S(2)}) async-start(bf16[64,4,512]{2,0,1:T(8,128)(2,1)} %bitcast.108), calls=%async_computation.2 | async-start | bytes 524288 | tf_op jit(solution)/shard_map/all_to_all | solution.py:43
  32.5 153.2 %reduce-scatter.2.cloned.1.call-start = ((), (), s32[]{:S(2)}) async-start(), calls=%async_computation.8 | async-start | bytes 2359296 | tf_op jit(solution)/shard_map/reduce_scatter | solution.py:170
  63.7 3.3 %copy-start = (bf16[8,1024,256]{2,1,0:T(8,128)(2,1)S(1)}, bf16[8,1024,256]{2,1,0:T(8,128)(2,1)}, u32[]{:S(2)}) copy-start(bf16[8,1024,256]{2,1,0:T(8,128)(2,1)} %reshape.329) | copy-start | bytes 12582916 | tf_op jit(solution)/shard_map/while
  66.4 1.0 copy-start.1
  68.8 1.0 copy-start.4
  70.3 0.8 copy-start.5
  112.1 3.3 %copy-start = (bf16[8,1024,256]{2,1,0:T(8,128)(2,1)S(1)}, bf16[8,1024,256]{2,1,0:T(8,128)(2,1)}, u32[]{:S(2)}) copy-start(bf16[8,1024,256]{2,1,0:T(8,128)(2,1)} %reshape.329) | copy-start | bytes 12582916 | tf_op jit(solution)/shard_map/while
  114.8 1.0 copy-start.1
  117.2 1.0 copy-start.4
  118.7 0.8 copy-start.5
  150.1 0.9 copy-start.6
  155.0 9.4 %all-to-all-start.4 = ((bf16[4,2,16384]{2,1,0:T(2,128)(2,1)}), bf16[4,2,16384]{2,1,0:T(2,128)(2,1)S(1)}, u32[]{:S(2)}, u32[]{:S(2)}) async-start(bf16[4,2,16384]{2,1,0:T(2,128)(2,1)} %reshape.325), calls=%async_computation.4 | async-start | bytes 524288 | tf_op jit(solution)/shard_map/all_to_all | solution.py:166
  164.4 23.1 %all-to-all-start.3 = ((bf16[4,2,16384]{2,1,0:T(2,128)(2,1)}), bf16[4,2,16384]{2,1,0:T(2,128)(2,1)S(1)}, u32[]{:S(2)}, u32[]{:S(2)}) async-start(bf16[4,2,16384]{2,1,0:T(2,128)(2,1)} %reshape.323), calls=%async_computation.3 | async-start | bytes 524288 | tf_op jit(solution)/shard_map/all_to_all | solution.py:165
  187.5 9.1 %all-to-all-start.5 = ((f32[256,1,256]{2,1,0:T(1,128)}), f32[256,1,256]{2,1,0:T(1,128)S(1)}, u32[]{:S(2)}, u32[]{:S(2)}) async-start(f32[256,1,256]{2,1,0:T(1,128)} %reshape.311), calls=%async_computation.6 | async-start | bytes 524288 | tf_op jit(solution)/shard_map/all_to_all | solution.py:171
Sparse Core Ops, SparseCore 0:
  25.6 23.7 all-gather.1
  150.3 35.3 reduce-scatter.1
where the time goes:
time: 206 us; the launch traced here: 204 us
  local copies, waits for them, and re-layouts  79.7 us (39%)
  waiting for transfers between devices  38.1 us (18%)
  matrix products  33.1 us (16%)
  starting transfers between devices  23.5 us (11%)
  other arithmetic  15.2 us (7%)
  between operations  14.3 us (7%)
    reshape x2, local copies, waits for them, and re-layouts, group_step(): jnp.concatenate([key_portion, value_portion], axis=2)  18.7 us
    concatenate x2, local copies, waits for them, and re-layouts, group_step(): jnp.concatenate([key_portion, value_portion], axis=2)  18.3 us
    reduce_scatter x1, waiting for transfers between devices, body(): lax.psum_scatter(kv_grad_all, 'blk', scatter_dimension=0, tiled=True)  17.8 us
    reshape x2, local copies, waits for them, and re-layouts, group_step(): gathered = jnp.dot(fetch_table, keys_units, preferred_element_type=jnp.fl...  14.9 us
    dot_general x2, matrix products, group_step(): jnp.dot(place_table.T, both_parts, preferred_element_type=jnp.float32, pr...  11.3 us
    dot_general x2, matrix products, group_step(): jnp.dot(fetch_table, keys_units, preferred_element_type=jnp.float32)  8.93 us
    concatenate x2, other arithmetic, group_step(): jnp.concatenate([key_portion, value_portion], axis=2)  8.15 us
    all_gather x1, waiting for transfers between devices, body(): keys_all = lax.all_gather(kv_mine[:, 0, :], 'blk', axis=0, tiled=True)  8.01 us
  transfers between devices with their start and end apart: 8, of which 7 were waited for; matrix products, arithmetic and copies ran while one was open for 12% of the time, Pallas kernels for 0%

commit v1 on v0

v1 whole, which is shorter than its diff:
```python
import functools
import math

import jax
import jax.numpy as jnp
from jax import lax
from jax.experimental import pallas as pl
from jax.experimental.pallas import tpu as pltpu
from jax.sharding import PartitionSpec as P

KEY_VALUE_HEADS = 2
HEAD_SIZE = 128
BLOCK = 128
MESH = pl.DeviceIdType.MESH
VMEM_LIMIT = 56 * 1024 * 1024


def flip(u, mask, width):
    bit = 1
    while bit < width:
        if mask & bit:
            u = u + bit * (1 - 2 * ((u // bit) % 2))
        bit *= 2
    return u


def bits_of(width):
    return [1 << t for t in range(width.bit_length() - 1)]


def span(bits):
    masks = [0]
    for bit in bits:
        masks = masks + [m | bit for m in masks]
    return masks


def greet(width, chips, u, b, c, g):
    barrier = pltpu.get_barrier_semaphore()
    peers = [(u, c * 2 + (1 - g))]
    peers += [(u, ((c + d) % chips) * 2 + g) for d in range(1, chips)]
    peers += [(flip(u, m, width), b) for m in range(1, width)]
    for peer in peers:
        pl.semaphore_signal(barrier, inc=1, device_id=peer, device_id_type=MESH)
    pl.semaphore_wait(barrier, len(peers))


def remote(src, dst, send_sem, recv_sem, device):
    return pltpu.make_async_remote_copy(
        src_ref=src, dst_ref=dst, send_sem=send_sem, recv_sem=recv_sem,
        device_id=device, device_id_type=MESH,
    )


def gather_kernel(
    width, chips,
    q_ref, do_ref, k_ref, v_ref, list_ref,
    qx, dox, kall, vall, kt, vt, table,
    ks, kr, vs, vr, ts, tr, ps, pr,
):
    u, b = lax.axis_index("uly"), lax.axis_index("blk")
    c, g = b // 2, b % 2
    half = q_ref.shape[1] // 2
    seg = q_ref.shape[0]
    me = u * chips + c
    mine = pl.ds(pl.multiple_of(g * seg, seg), seg)
    my_head = pl.ds(pl.multiple_of(g * HEAD_SIZE, HEAD_SIZE), HEAD_SIZE)
    other_head = pl.ds(pl.multiple_of((1 - g) * HEAD_SIZE, HEAD_SIZE), HEAD_SIZE)
    my_half = pl.ds(pl.multiple_of(g * half, half), half)
    other_half = pl.ds(pl.multiple_of((1 - g) * half, half), half)
    sibling = (u, c * 2 + (1 - g))

    kall[me, mine, :] = k_ref[:, my_head]
    vall[me, mine, :] = v_ref[:, my_head]
    table[u] = list_ref[...]
    greet(width, chips, u, b, c, g)

    started = []

    def start(copy):
        copy.start()
        started.append(copy)
        return copy

    pair = [
        start(remote(k_ref.at[:, other_head], kall.at[me, mine, :], ps.at[0], pr.at[0], sibling)),
        start(remote(v_ref.at[:, other_head], vall.at[me, mine, :], ps.at[1], pr.at[1], sibling)),
        start(remote(q_ref.at[:, other_half], qx.at[mine, :], ps.at[2], pr.at[2], sibling)),
        start(remote(do_ref.at[:, other_half], dox.at[mine, :], ps.at[3], pr.at[3], sibling)),
    ]
    tables = [
        start(remote(list_ref, table.at[u], ts.at[m], tr.at[m], (flip(u, m, width), b)))
        for m in range(1, width)
    ]
    qx[mine, :] = q_ref[:, my_half]
    dox[mine, :] = do_ref[:, my_half]

    def place(m, d):
        return flip(u, m, width) * chips + (c + d) % chips

    orders = (bits_of(width), bits_of(width)[::-1])
    arrays = ((kall, ks, kr, kt), (vall, vs, vr, vt))

    def forward(which, m, d):
        ref, send, recv, _ = arrays[which]
        order = orders[which]
        at = place(m, d)
        if m == 0 and d == 0:
            for e in range(1, chips):
                peer = (u, ((c + e) % chips) * 2 + g)
                start(remote(ref.at[at], ref.at[at], send.at[e], recv.at[(chips - e) % chips], peer))
        last = max([t for t, bit in enumerate(order) if m & bit], default=-1)
        for bit in order[last + 1:]:
            slot = (m ^ bit) * chips + d
            peer = (flip(u, bit, width), b)
            start(remote(ref.at[at], ref.at[at], send.at[slot], recv.at[slot], peer))

    def arrived(which, m, d):
        ref, send, recv, _ = arrays[which]
        at = place(m, d)
        slot = m * chips + d
        remote(ref.at[at], ref.at[at], send.at[slot], recv.at[slot], sibling).wait_recv()

    def turn(which, m, d):
        ref, _, _, turned = arrays[which]
        at = place(m, d)
        turned[at] = ref[at].T

    items = sorted(
        ((m, d) for m in range(width) for d in range(chips)),
        key=lambda item: (item[1] + 1.1 * bin(item[0]).count("1"), item[0]),
    )
    pair[0].wait_recv()
    forward(0, 0, 0)
    pair[1].wait_recv()
    forward(1, 0, 0)
    turn(0, 0, 0)
    turn(1, 0, 0)
    for m, d in items:
        if m == 0 and d == 0:
            continue
        for which in (0, 1):
            arrived(which, m, d)
            forward(which, m, d)
        for which in (0, 1):
            turn(which, m, d)
    pair[2].wait_recv()
    pair[3].wait_recv()
    for copy in tables:
        copy.wait_recv()
    for copy in started:
        copy.wait_send()


def attention_kernel(
    chips, heads, list_len,
    table, qx, dox, kall, vall, kt, vt,
    outx, dqx, gk, gv,
    names, kacc, vacc,
):
    u, b = lax.axis_index("uly"), lax.axis_index("blk")
    g = b % 2
    block = u * chips + b // 2
    blocks = kall.shape[0]
    per_shard = table.shape[1]
    scale = 1.0 / math.sqrt(HEAD_SIZE)
    log2e = math.log2(math.e)

    def clear(j, carry):
        kacc[j] = jnp.zeros((BLOCK, HEAD_SIZE), jnp.float32)
        vacc[j] = jnp.zeros((BLOCK, HEAD_SIZE), jnp.float32)
        return carry

    lax.fori_loop(0, blocks, clear, 0)

    def work(n, columns):
        at = [names[t] for t in range(n)]
        q = qx[:, columns]
        do = dox[:, columns]
        keys = jnp.concatenate([kall[e] for e in at], axis=0)
        values = jnp.concatenate([vall[e] for e in at], axis=0)
        contract = (((1,), (1,)), ((), ()))
        scores = lax.dot_general(keys, q, contract, preferred_element_type=jnp.float32)
        scores = scores * (scale * log2e)
        row = lax.broadcasted_iota(jnp.int32, (BLOCK, BLOCK), 0)
        col = lax.broadcasted_iota(jnp.int32, (BLOCK, BLOCK), 1)
        head_part = jnp.where(row <= col, scores[:BLOCK], -1e30)
        scores = jnp.concatenate([head_part, scores[BLOCK:]], axis=0) if n > 1 else head_part
        top = jnp.max(scores, axis=0, keepdims=True)
        powers = jnp.exp2(scores - top)
        weights = powers * (1.0 / jnp.sum(powers, axis=0, keepdims=True))
        low = weights.astype(jnp.bfloat16)
        grad_weights = lax.dot_general(values, do, contract, preferred_element_type=jnp.float32)
        row_dot = jnp.sum(weights * grad_weights, axis=0, keepdims=True)
        score_grad = (weights * (grad_weights - row_dot) * scale).astype(jnp.bfloat16)
        values_t = jnp.concatenate([vt[e] for e in at], axis=1)
        keys_t = jnp.concatenate([kt[e] for e in at], axis=1)
        out_t = jnp.dot(values_t, low, preferred_element_type=jnp.float32)
        dq_t = jnp.dot(keys_t, score_grad, preferred_element_type=jnp.float32)
        outx[:, columns] = out_t.T.astype(jnp.bfloat16)
        dqx[:, columns] = dq_t.T.astype(jnp.bfloat16)
        dv = jnp.dot(low, do, preferred_element_type=jnp.float32)
        dk = jnp.dot(score_grad, q, preferred_element_type=jnp.float32)
        for t, e in enumerate(at):
            kacc[e] += dk[t * BLOCK:(t + 1) * BLOCK]
            vacc[e] += dv[t * BLOCK:(t + 1) * BLOCK]

    def head_step(h, carry):
        head = g * heads + h
        shard, local = head // per_shard, head % per_shard
        count = jnp.int32(1)
        names[0] = block
        for t in range(1, list_len):
            entry = table[shard, local, block * list_len + t]
            names[count] = entry
            count = count + jnp.where(entry < blocks, 1, 0).astype(jnp.int32)
        columns = pl.ds(pl.multiple_of(h * HEAD_SIZE, HEAD_SIZE), HEAD_SIZE)
        for n in range(1, list_len + 1):
            pl.when(count == n)(functools.partial(work, n, columns))
        return carry

    lax.fori_loop(0, heads, head_step, 0)

    def finish(j, carry):
        gk[j] = kacc[j].astype(jnp.bfloat16)
        gv[j] = vacc[j].astype(jnp.bfloat16)
        return carry

    lax.fori_loop(0, blocks, finish, 0)


def scatter_kernel(
    width, chips,
    outx, dqx, gk, gv,
    out, dq, out_k, out_v,
    rk, rv, ak, av, fk, fv,
    ks, kr, vs, vr, ps, pr,
):
    u, b = lax.axis_index("uly"), lax.axis_index("blk")
    c, g = b // 2, b % 2
    half = outx.shape[1]
    seg = out.shape[0]
    mine = pl.ds(pl.multiple_of(g * seg, seg), seg)
    theirs = pl.ds(pl.multiple_of((1 - g) * seg, seg), seg)
    my_head = pl.ds(pl.multiple_of(g * HEAD_SIZE, HEAD_SIZE), HEAD_SIZE)
    my_half = pl.ds(pl.multiple_of(g * half, half), half)
    sibling = (u, c * 2 + (1 - g))
    greet(width, chips, u, b, c, g)
    started = []

    def start(copy):
        copy.start()
        started.append(copy)
        return copy

    def place(m, d):
        return flip(u, m, width) * chips + (c + d) % chips

    orders = (bits_of(width)[::-1], bits_of(width))
    arrays = ((gk, rk, ak, ks, kr), (gv, rv, av, vs, vr))
    stages = len(orders[0])
    bases = []
    total = 0
    for t in range(stages):
        bases.append(total)
        total += (width >> (t + 1)) * chips
    line = total
    ranked = [
        [sorted(span(order[t + 1:]), key=lambda m: -bin(m).count("1")) for t in range(stages)]
        for order in orders
    ]

    def slot(which, t, s, d):
        return bases[t] + ranked[which][t].index(s) * chips + d

    def current(which, t, m, d):
        grads, _, sums, _, _ = arrays[which]
        if t == 0:
            return grads.at[place(m, d)]
        return sums.at[slot(which, t - 1, m, d)]

    def send(which, t, s, d):
        _, landing, _, ssem, rsem = arrays[which]
        bit = orders[which][t]
        at = slot(which, t, s, d)
        start(remote(
            current(which, t, s ^ bit, d), landing.at[at], ssem.at[at], rsem.at[at],
            (flip(u, bit, width), b),
        ))

    line_order = list(range(1, chips)) + [0]
    for t_s in range(width // 2):
        for d in line_order:
            for which in (0, 1):
                send(which, 0, ranked[which][0][t_s], d)
    pair = [
        start(remote(outx.at[theirs, :], out.at[:, my_half], ps.at[0], pr.at[0], sibling)),
        start(remote(dqx.at[theirs, :], dq.at[:, my_half], ps.at[1], pr.at[1], sibling)),
    ]
    out[:, my_half] = outx[mine, :]
    dq[:, my_half] = dqx[mine, :]

    for t in range(stages):
        for s_at in range(len(ranked[0][t])):
            for d in line_order:
                for which in (0, 1):
                    _, landing, sums, ssem, rsem = arrays[which]
                    s = ranked[which][t][s_at]
                    at = slot(which, t, s, d)
                    remote(
                        landing.at[at], landing.at[at], ssem.at[at], rsem.at[at], sibling
                    ).wait_recv()
                    own = current(which, t, s, d)
                    sums[at] = (
                        own[...].astype(jnp.float32) + landing[at].astype(jnp.float32)
                    ).astype(jnp.bfloat16)
                    if t + 1 < stages:
                        if s & orders[which][t + 1]:
                            send(which, t + 1, s ^ orders[which][t + 1], d)
                    elif d:
                        start(remote(
                            sums.at[at], landing.at[line + (chips - d) % chips],
                            ssem.at[line + d], rsem.at[line + (chips - d) % chips],
                            (u, ((c + d) % chips) * 2 + g),
                        ))
    finals = ((fk, out_k), (fv, out_v))
    last = []
    for which in (0, 1):
        _, landing, sums, ssem, rsem = arrays[which]
        result, target = finals[which]
        value = sums[slot(which, stages - 1, 0, 0)].astype(jnp.float32)
        for d in range(1, chips):
            at = line + d
            remote(landing.at[at], landing.at[at], ssem.at[at], rsem.at[at], sibling).wait_recv()
            value = value + landing[at].astype(jnp.float32)
        result[...] = value.astype(jnp.bfloat16)
        last.append(start(remote(
            result.at[theirs, :], target.at[:, my_head], ps.at[2 + which], pr.at[2 + which], sibling
        )))
        target[:, my_head] = result[mine, :]
    for copy in pair + last:
        copy.wait_recv()
    for copy in started:
        copy.wait_send()


def body(queries, key_rows, value_rows, out_grad, block_list):
    width = lax.axis_size("uly")
    chips = lax.axis_size("blk") // 2
    seg, columns = queries.shape
    heads_dev, blocks, list_len = block_list.shape
    heads = heads_dev * width // KEY_VALUE_HEADS
    half = columns // 2
    low = jnp.bfloat16
    vmem = pl.BlockSpec(memory_space=pltpu.VMEM)
    smem = pl.BlockSpec(memory_space=pltpu.SMEM)
    dma = pltpu.SemaphoreType.DMA

    earlier = jnp.arange(list_len)[:, None] > jnp.arange(list_len)[None, :]
    repeated = jnp.any(
        (block_list[:, :, :, None] == block_list[:, :, None, :]) & earlier[None, None], axis=3
    )
    lists = jnp.where(repeated, blocks, block_list).reshape(heads_dev, blocks * list_len)

    cube = jax.ShapeDtypeStruct((blocks, BLOCK, HEAD_SIZE), low)
    wide = jax.ShapeDtypeStruct((BLOCK, half), low)
    qx, dox, kall, vall, kt, vt, table = pl.pallas_call(
        functools.partial(gather_kernel, width, chips),
        out_shape=(
            wide, wide, cube, cube, cube, cube,
            jax.ShapeDtypeStruct((width, heads_dev, blocks * list_len), jnp.int32),
        ),
        in_specs=[vmem] * 5,
        out_specs=(vmem,) * 7,
        scratch_shapes=[dma((width * chips,))] * 4 + [dma((width,))] * 2 + [dma((4,))] * 2,
        compiler_params=pltpu.CompilerParams(
            collective_id=0, has_side_effects=True, vmem_limit_bytes=VMEM_LIMIT
        ),
        name="gather",
    )(queries, out_grad, key_rows, value_rows, lists)

    outx, dqx, gk, gv = pl.pallas_call(
        functools.partial(attention_kernel, chips, heads, list_len),
        out_shape=(wide, wide, cube, cube),
        in_specs=[smem] + [vmem] * 6,
        out_specs=(vmem,) * 4,
        scratch_shapes=[
            pltpu.SMEM((list_len + 1,), jnp.int32),
            pltpu.VMEM((blocks, BLOCK, HEAD_SIZE), jnp.float32),
            pltpu.VMEM((blocks, BLOCK, HEAD_SIZE), jnp.float32),
        ],
        compiler_params=pltpu.CompilerParams(vmem_limit_bytes=VMEM_LIMIT),
        name="attention",
    )(table, qx, dox, kall, vall, kt, vt)

    slots = width * chips
    landing = pltpu.VMEM((slots, BLOCK, HEAD_SIZE), low)
    return pl.pallas_call(
        functools.partial(scatter_kernel, width, chips),
        out_shape=(
            jax.ShapeDtypeStruct((seg, columns), low),
            jax.ShapeDtypeStruct((seg, columns), low),
            jax.ShapeDtypeStruct((seg, KEY_VALUE_HEADS * HEAD_SIZE), low),
            jax.ShapeDtypeStruct((seg, KEY_VALUE_HEADS * HEAD_SIZE), low),
        ),
        in_specs=[vmem] * 4,
        out_specs=(vmem,) * 4,
        scratch_shapes=[landing] * 4
        + [pltpu.VMEM((BLOCK, HEAD_SIZE), low)] * 2
        + [dma((slots,))] * 4
        + [dma((4,))] * 2,
        compiler_params=pltpu.CompilerParams(
            collective_id=1, has_side_effects=True, vmem_limit_bytes=VMEM_LIMIT
        ),
        name="scatter",
    )(outx, dqx, gk, gv)


def solution(mesh):
    rows = P(("uly", "blk"), None)
    return jax.shard_map(
        body,
        mesh=mesh,
        in_specs=(rows, rows, rows, rows, P("uly", None, None)),
        out_specs=(rows, rows, rows, rows),
        check_vma=False,
    )
```

time: 206 us -> 61.4 us (0.30)
  local copies, waits for them, and re-layouts: 79.7 us -> 4.61 us
  Pallas kernels: 0 us -> 54.5 us
  waiting for transfers between devices: 38.1 us -> 0 us
  matrix products: 33.1 us -> 0 us
  starting transfers between devices: 23.5 us -> 0 us
  other arithmetic: 15.2 us -> 0.95 us
  between operations: 14.3 us -> 0.69 us
    pallas_call x0 -> x3, Pallas kernels: none -> 54.5 us  [the longest x1 25.5 us: body(): pl.pallas_call(functools.partial(gather_kernel, width, chips), out_shape=...]
    reshape x18 -> x1, local copies, waits for them, and re-layouts: 47.9 us -> 0.68 us  [body(): jnp.where(repeated, blocks, block_list)]
    dot_general x16 -> x0, matrix products: 33.1 us -> none  [the longest x2 11.3 us: group_step(): jnp.dot(place_table.T, both_parts, preferred_element_type=jnp.float32, pr...]
    all_to_all x6 -> x0, starting transfers between devices: 23.4 us -> none  [the longest x1 5.16 us: body(): lax.all_to_all(kv_slots, 'uly', split_axis=1, concat_axis=0, tiled=True)]
    concatenate x3 -> x0, local copies, waits for them, and re-layouts: 18.3 us -> none  [the longest x2 18.3 us: group_step(): jnp.concatenate([key_portion, value_portion], axis=2)]
    reduce_scatter x1 -> x0, waiting for transfers between devices: 17.8 us -> none  [body(): lax.psum_scatter(kv_grad_all, 'blk', scatter_dimension=0, tiled=True)]
    all_to_all x6 -> x0, waiting for transfers between devices: 11.6 us -> none  [the longest x1 3.34 us: body(): lax.all_to_all(kv_slots, 'uly', split_axis=1, concat_axis=0, tiled=True)]
    concatenate x4 -> x0, other arithmetic: 8.23 us -> none  [the longest x2 8.15 us: group_step(): jnp.concatenate([key_portion, value_portion], axis=2)]
  transfers between devices with their start and end apart: 8 -> 0, of which waited for: 7 -> 0; matrix products, arithmetic and copies ran while one was open for 12% -> 0% of each run, Pallas kernels for 0% -> 0%
where the time goes in v1:
time: 61.4 us; the launch traced here: 60.8 us
  Pallas kernels  54.5 us (89%)
  local copies, waits for them, and re-layouts  4.61 us (8%)
  other arithmetic  0.95 us (2%)
  between operations  0.69 us (1%)
    pallas_call x1, Pallas kernels, body(): pl.pallas_call(functools.partial(gather_kernel, width, chips), out_shape=...  25.5 us
    pallas_call x1, Pallas kernels, body(): pl.pallas_call(functools.partial(scatter_kernel, width, chips), out_shape...  21.4 us
    pallas_call x1, Pallas kernels, body(): pl.pallas_call(functools.partial(attention_kernel, chips, heads, list_len...  7.61 us
    unnamed x12, local copies, waits for them, and re-layouts  3.86 us

profile of v1, /device:TPU:0, one launch (start us, length us, event | category | flops | bytes accessed | tf_op | source)
XLA Modules:
  0.0 60.8 jit_solution(16483647450951466554)
XLA Ops:
  0.6 0.0 copy-start.1
  0.7 0.9 %and_reduce_fusion = pred[4,16,8]{1,2,0:T(8,128)(4,1)S(1)} fusion(s32[4,16,8]{1,2,0:T(8,128)} %param.9, pred[8,8]{1,0:T(8,128)(4,1)S(1)} %iota_compare_fusion), kind=kLoop, calls=%fused_computation | loop fusion | flops 11776 | bytes 2624 | tf_op jit(solution)/shard_map/reduce_or | solution.py:360
  1.6 0.0 copy-done.1
  1.6 0.1 copy.15
  1.7 0.7 %reshape.25.list_ref = s32[4,128]{1,0:T(4,128)} reshape(s32[4,16,8]{2,1,0:T(8,128)S(1)} %copy.15) | data formatting | bytes 4096 | tf_op jit(solution)/shard_map/reshape | solution.py:363
  2.4 25.5 %gather.1 = (bf16[128,1024]{1,0:T(8,128)(2,1)}, bf16[128,1024]{1,0:T(8,128)(2,1)}, bf16[16,128,128]{2,1,0:T(8,128)(2,1)}, bf16[16,128,128]{2,1,0:T(8,128)(2,1)},...) custom-call(bf16[64,2048]{1,0:T(8,128)(2,1)} %q_ref.1, ...), custom_call_target="tpu_custom_call" | custom-call | tf_op jit(solution)/shard_map/gather/pallas_call | solution.py:367
  27.9 7.6 %attention.1 = (bf16[128,1024]{1,0:T(8,128)(2,1)}, bf16[128,1024]{1,0:T(8,128)(2,1)}, bf16[16,128,128]{2,1,0:T(8,128)(2,1)}, bf16[16,128,128]{2,1,0:T(8,128)(2,1)}) custom-call(s32[4,4,128]{2,1,0:T(4,128)} %get-tuple-element.15.table, bf16[128,1024]{1,0:T(8,128)(2,1)} %get-tuple-element.16.qx, bf16[128,1024]{1,0:T(8,128)(2,1)} %get-tuple-element.17.dox, ...), custom_call_target="tpu_custom_call" | custom-call | tf_op jit(solution)/shard_map/attention/pallas_call | solution.py:382
  35.5 21.4 %scatter.1 = (bf16[64,2048]{1,0:T(8,128)(2,1)}, bf16[64,2048]{1,0:T(8,128)(2,1)}, bf16[64,256]{1,0:T(8,128)(2,1)}, bf16[64,256]{1,0:T(8,128)(2,1)}) custom-call(bf16[128,1024]{1,0:T(8,128)(2,1)} %get-tuple-element.22.outx, bf16[128,1024]{1,0:T(8,128)(2,1)} %get-tuple-element.23.dqx, bf16[16,128,128]{2,1,0:T(8,128)(2,1)} %get-tuple-element.24.gk, ...), custom_call_target="tpu_custom_call" | custom-call | tf_op jit(solution)/shard_map/scatter/pallas_call | solution.py:398
  56.9 0.0 copy-start
  56.9 1.7 %copy.20 = bf16[64,2048]{1,0:T(8,128)(2,1)} copy(bf16[64,2048]{1,0:T(8,128)(2,1)} %get-tuple-element.30) | data formatting | bytes 524288
  58.6 0.0 copy-done
  58.6 0.0 copy-start.3
  58.6 0.7 %copy.21 = bf16[64,2048]{1,0:T(8,128)(2,1)} copy(bf16[64,2048]{1,0:T(8,128)(2,1)S(1)} %copy-done) | data formatting | bytes 524288
  59.3 0.1 copy-done.3
  59.4 0.0 copy-start.2
  59.4 0.6 %copy.22 = bf16[64,256]{1,0:T(8,128)(2,1)} copy(bf16[64,256]{1,0:T(8,128)(2,1)S(1)} %copy-done.3) | data formatting | bytes 65536
  60.0 0.2 copy-done.2
  60.2 0.6 %copy.23 = bf16[64,256]{1,0:T(8,128)(2,1)} copy(bf16[64,256]{1,0:T(8,128)(2,1)S(1)} %copy-done.2) | data formatting | bytes 65536
  (2 shorter events, 0.0 us)
Async XLA Ops:
  0.6 1.0 %copy-start.1 = (s32[4,16,8]{1,2,0:T(8,128)S(1)}, s32[4,16,8]{1,2,0:T(8,128)}, u32[]{:S(2)}) copy-start(s32[4,16,8]{1,2,0:T(8,128)} %param.9) | copy-start | bytes 6148
  56.9 1.7 %copy-start = (bf16[64,2048]{1,0:T(8,128)(2,1)S(1)}, bf16[64,2048]{1,0:T(8,128)(2,1)}, u32[]{:S(2)}) copy-start(bf16[64,2048]{1,0:T(8,128)(2,1)} %get-tuple-element.31) | copy-start | bytes 786436
  58.6 0.8 %copy-start.3 = (bf16[64,256]{1,0:T(8,128)(2,1)S(1)}, bf16[64,256]{1,0:T(8,128)(2,1)}, u32[]{:S(2)}) copy-start(bf16[64,256]{1,0:T(8,128)(2,1)} %get-tuple-element.32) | copy-start | bytes 98308
  59.4 0.8 %copy-start.2 = (bf16[64,256]{1,0:T(8,128)(2,1)S(1)}, bf16[64,256]{1,0:T(8,128)(2,1)}, u32[]{:S(2)}) copy-start(bf16[64,256]{1,0:T(8,128)(2,1)} %get-tuple-element.33) | copy-start | bytes 98308

commit v2 on v1

--- a/solution.py
+++ b/solution.py
@@ -21,6 +21,12 @@
         if mask & bit:
             u = u + bit * (1 - 2 * ((u // bit) % 2))
         bit *= 2
+    return u
+
+
+def top(u, bits):
+    for bit in bits:
+        u = u + bit * (1 - (u // bit) % 2)
     return u
 
 
@@ -77,23 +83,18 @@
 
     started = []
 
-    def start(copy):
-        copy.start()
-        started.append(copy)
+    def start(copy, needed=None):
+        if needed is None:
+            copy.start()
+        else:
+            pl.when(needed)(copy.start)
+        started.append((copy, needed))
         return copy
 
     pair = [
         start(remote(k_ref.at[:, other_head], kall.at[me, mine, :], ps.at[0], pr.at[0], sibling)),
         start(remote(v_ref.at[:, other_head], vall.at[me, mine, :], ps.at[1], pr.at[1], sibling)),
-        start(remote(q_ref.at[:, other_half], qx.at[mine, :], ps.at[2], pr.at[2], sibling)),
-        start(remote(do_ref.at[:, other_half], dox.at[mine, :], ps.at[3], pr.at[3], sibling)),
-    ]
-    tables = [
-        start(remote(list_ref, table.at[u], ts.at[m], tr.at[m], (flip(u, m, width), b)))
-        for m in range(1, width)
-    ]
-    qx[mine, :] = q_ref[:, my_half]
-    dox[mine, :] = do_ref[:, my_half]
+    ]
 
     def place(m, d):
         return flip(u, m, width) * chips + (c + d) % chips
@@ -101,55 +102,91 @@
     orders = (bits_of(width), bits_of(width)[::-1])
     arrays = ((kall, ks, kr, kt), (vall, vs, vr, vt))
 
+    def later(which, m):
+        order = orders[which]
+        return order[max([t for t, bit in enumerate(order) if m & bit], default=-1) + 1:]
+
+    def wanted(which, m, d):
+        return place(m, d) <= top(u, later(which, m)) * chips + c
+
     def forward(which, m, d):
         ref, send, recv, _ = arrays[which]
-        order = orders[which]
         at = place(m, d)
         if m == 0 and d == 0:
             for e in range(1, chips):
-                peer = (u, ((c + e) % chips) * 2 + g)
-                start(remote(ref.at[at], ref.at[at], send.at[e], recv.at[(chips - e) % chips], peer))
-        last = max([t for t, bit in enumerate(order) if m & bit], default=-1)
-        for bit in order[last + 1:]:
+                there = (c + e) % chips
+                start(
+                    remote(
+                        ref.at[at], ref.at[at], send.at[e], recv.at[(chips - e) % chips],
+                        (u, there * 2 + g),
+                    ),
+                    at <= (width - 1) * chips + there,
+                )
+        for bit in later(which, m):
             slot = (m ^ bit) * chips + d
-            peer = (flip(u, bit, width), b)
-            start(remote(ref.at[at], ref.at[at], send.at[slot], recv.at[slot], peer))
+            u_there = flip(u, bit, width)
+            start(
+                remote(ref.at[at], ref.at[at], send.at[slot], recv.at[slot], (u_there, b)),
+                at <= top(u_there, later(which, m ^ bit)) * chips + c,
+            )
 
     def arrived(which, m, d):
         ref, send, recv, _ = arrays[which]
         at = place(m, d)
         slot = m * chips + d
-        remote(ref.at[at], ref.at[at], send.at[slot], recv.at[slot], sibling).wait_recv()
+        copy = remote(ref.at[at], ref.at[at], send.at[slot], recv.at[slot], sibling)
+        pl.when(wanted(which, m, d))(copy.wait_recv)
 
     def turn(which, m, d):
         ref, _, _, turned = arrays[which]
         at = place(m, d)
-        turned[at] = ref[at].T
-
-    items = sorted(
-        ((m, d) for m in range(width) for d in range(chips)),
-        key=lambda item: (item[1] + 1.1 * bin(item[0]).count("1"), item[0]),
-    )
+
+        @pl.when(at <= me)
+        def _():
+            turned[at] = ref[at].T
+
+    items = [
+        (which, m, d)
+        for m in range(width) for d in range(chips) for which in (0, 1)
+        if (m, d) != (0, 0)
+    ]
+    items.sort(key=lambda item: (
+        not later(item[0], item[1]), item[2] + 1.1 * bin(item[1]).count("1")
+    ))
     pair[0].wait_recv()
     forward(0, 0, 0)
     pair[1].wait_recv()
     forward(1, 0, 0)
-    turn(0, 0, 0)
-    turn(1, 0, 0)
-    for m, d in items:
-        if m == 0 and d == 0:
-            continue
-        for which in (0, 1):
-            arrived(which, m, d)
-            forward(which, m, d)
-        for which in (0, 1):
-            turn(which, m, d)
+    pair += [
+        start(remote(q_ref.at[:, other_half], qx.at[mine, :], ps.at[2], pr.at[2], sibling)),
+        start(remote(do_ref.at[:, other_half], dox.at[mine, :], ps.at[3], pr.at[3], sibling)),
+    ]
+    tables = [
+        start(remote(list_ref, table.at[u], ts.at[m], tr.at[m], (flip(u, m, width), b)))
+        for m in range(1, width)
+    ]
+    qx[mine, :] = q_ref[:, my_half]
+    dox[mine, :] = do_ref[:, my_half]
+    handed_on = [item for item in items if later(item[0], item[1])]
+    for item in handed_on:
+        arrived(*item)
+        forward(*item)
+    for which in (0, 1):
+        turn(which, 0, 0)
+    for item in handed_on:
+        turn(*item)
+    for item in items[len(handed_on):]:
+        arrived(*item)
+        turn(*item)
     pair[2].wait_recv()
     pair[3].wait_recv()
     for copy in tables:
         copy.wait_recv()
-    for copy in started:
-        copy.wait_send()
+    for copy, needed in started:
+        if needed is None:
+            copy.wait_send()
+        else:
+            pl.when(needed)(copy.wait_send)
 
 
 def attention_kernel(
@@ -248,9 +285,12 @@
     greet(width, chips, u, b, c, g)
     started = []
 
-    def start(copy):
-        copy.start()
-        started.append(copy)
+    def start(copy, needed=None):
+        if needed is None:
+            copy.start()
+        else:
+            pl.when(needed)(copy.start)
+        started.append((copy, needed))
         return copy
 
     def place(m, d):
@@ -283,10 +323,22 @@
         _, landing, _, ssem, rsem = arrays[which]
         bit = orders[which][t]
         at = slot(which, t, s, d)
-        start(remote(
-            current(which, t, s ^ bit, d), landing.at[at], ssem.at[at], rsem.at[at],
-            (flip(u, bit, width), b),
-        ))
+        start(
+            remote(
+                current(which, t, s ^ bit, d), landing.at[at], ssem.at[at], rsem.at[at],
+                (flip(u, bit, width), b),
+            ),
+            place(s ^ bit, d) <= top(u, orders[which][:t]) * chips + c,
+        )
+
+    def receive(which, at, needed):
+        _, landing, _, ssem, rsem = arrays[which]
+        copy = remote(landing.at[at], landing.at[at], ssem.at[at], rsem.at[at], sibling)
+        pl.when(needed)(copy.wait_recv)
+
+        @pl.when(jnp.logical_not(needed))
+        def _():
+            landing[at] = jnp.zeros((BLOCK, HEAD_SIZE), landing.dtype)
 
     line_order = list(range(1, chips)) + [0]
     for t_s in range(width // 2):
@@ -307,9 +359,9 @@
                     _, landing, sums, ssem, rsem = arrays[which]
                     s = ranked[which][t][s_at]
                     at = slot(which, t, s, d)
-                    remote(
-                        landing.at[at], landing.at[at], ssem.at[at], rsem.at[at], sibling
-                    ).wait_recv()
+                    u_there = flip(u, orders[which][t], width)
+                    reach = top(u_there, orders[which][:t]) * chips + c
+                    receive(which, at, place(s, d) <= reach)
                     own = current(which, t, s, d)
                     sums[at] = (
                         own[...].astype(jnp.float32) + landing[at].astype(jnp.float32)
@@ -318,11 +370,14 @@
                         if s & orders[which][t + 1]:
                             send(which, t + 1, s ^ orders[which][t + 1], d)
                     elif d:
-                        start(remote(
-                            sums.at[at], landing.at[line + (chips - d) % chips],
-                            ssem.at[line + d], rsem.at[line + (chips - d) % chips],
-                            (u, ((c + d) % chips) * 2 + g),
-                        ))
+                        start(
+                            remote(
+                                sums.at[at], landing.at[line + (chips - d) % chips],
+                                ssem.at[line + d], rsem.at[line + (chips - d) % chips],
+                                (u, ((c + d) % chips) * 2 + g),
+                            ),
+                            place(0, d) <= (width - 1) * chips + c,
+                        )
     finals = ((fk, out_k), (fv, out_v))
     last = []
     for which in (0, 1):
@@ -331,7 +386,7 @@
         value = sums[slot(which, stages - 1, 0, 0)].astype(jnp.float32)
         for d in range(1, chips):
             at = line + d
-            remote(landing.at[at], landing.at[at], ssem.at[at], rsem.at[at], sibling).wait_recv()
+            receive(which, at, u * chips + c <= (width - 1) * chips + (c + d) % chips)
             value = value + landing[at].astype(jnp.float32)
         result[...] = value.astype(jnp.bfloat16)
         last.append(start(remote(
@@ -340,8 +395,11 @@
         target[:, my_head] = result[mine, :]
     for copy in pair + last:
         copy.wait_recv()
-    for copy in started:
-        copy.wait_send()
+    for copy, needed in started:
+        if needed is None:
+            copy.wait_send()
+        else:
+            pl.when(needed)(copy.wait_send)
 
 
 def body(queries, key_rows, value_rows, out_grad, block_list):

time: 61.4 us -> 60.7 us (0.989)
  Pallas kernels: 54.5 us -> 53.8 us
    pallas_call x1, Pallas kernels: 25.5 us -> 21.2 us  [body(): pl.pallas_call(functools.partial(gather_kernel, width, chips), out_shape=...]
    pallas_call x1, Pallas kernels: 21.4 us -> 25.1 us  [body(): pl.pallas_call(functools.partial(scatter_kernel, width, chips), out_shape...]
where the time goes in v2:
time: 60.7 us; the launch traced here: 60.1 us
  Pallas kernels  53.8 us (89%)
  local copies, waits for them, and re-layouts  4.61 us (8%)
  other arithmetic  0.95 us (2%)
  between operations  0.69 us (1%)
    pallas_call x1, Pallas kernels, body(): pl.pallas_call(functools.partial(scatter_kernel, width, chips), out_shape...  25.1 us
    pallas_call x1, Pallas kernels, body(): pl.pallas_call(functools.partial(gather_kernel, width, chips), out_shape=...  21.2 us
    pallas_call x1, Pallas kernels, body(): pl.pallas_call(functools.partial(attention_kernel, chips, heads, list_len...  7.6 us
    unnamed x12, local copies, waits for them, and re-layouts  3.86 us

profile of v2, /device:TPU:0, one launch (start us, length us, event | category | flops | bytes accessed | tf_op | source)
XLA Modules:
  0.0 60.1 jit_solution(10680291459300146907)
XLA Ops:
  0.6 0.0 copy-start.1
  0.7 0.9 %and_reduce_fusion = pred[4,16,8]{1,2,0:T(8,128)(4,1)S(1)} fusion(s32[4,16,8]{1,2,0:T(8,128)} %param.9, pred[8,8]{1,0:T(8,128)(4,1)S(1)} %iota_compare_fusion), kind=kLoop, calls=%fused_computation | loop fusion | flops 11776 | bytes 2624 | tf_op jit(solution)/shard_map/reduce_or | solution.py:418
  1.6 0.0 copy-done.1
  1.6 0.1 copy.15
  1.7 0.7 %reshape.25.list_ref = s32[4,128]{1,0:T(4,128)} reshape(s32[4,16,8]{2,1,0:T(8,128)S(1)} %copy.15) | data formatting | bytes 4096 | tf_op jit(solution)/shard_map/reshape | solution.py:421
  2.4 21.2 %gather.1 = (bf16[128,1024]{1,0:T(8,128)(2,1)}, bf16[128,1024]{1,0:T(8,128)(2,1)}, bf16[16,128,128]{2,1,0:T(8,128)(2,1)}, bf16[16,128,128]{2,1,0:T(8,128)(2,1)},...) custom-call(bf16[64,2048]{1,0:T(8,128)(2,1)} %q_ref.1, ...), custom_call_target="tpu_custom_call" | custom-call | tf_op jit(solution)/shard_map/gather/pallas_call | solution.py:425
  23.6 7.6 %attention.1 = (bf16[128,1024]{1,0:T(8,128)(2,1)}, bf16[128,1024]{1,0:T(8,128)(2,1)}, bf16[16,128,128]{2,1,0:T(8,128)(2,1)}, bf16[16,128,128]{2,1,0:T(8,128)(2,1)}) custom-call(s32[4,4,128]{2,1,0:T(4,128)} %get-tuple-element.15.table, bf16[128,1024]{1,0:T(8,128)(2,1)} %get-tuple-element.16.qx, bf16[128,1024]{1,0:T(8,128)(2,1)} %get-tuple-element.17.dox, ...), custom_call_target="tpu_custom_call" | custom-call | tf_op jit(solution)/shard_map/attention/pallas_call | solution.py:440
  31.2 25.1 %scatter.1 = (bf16[64,2048]{1,0:T(8,128)(2,1)}, bf16[64,2048]{1,0:T(8,128)(2,1)}, bf16[64,256]{1,0:T(8,128)(2,1)}, bf16[64,256]{1,0:T(8,128)(2,1)}) custom-call(bf16[128,1024]{1,0:T(8,128)(2,1)} %get-tuple-element.22.outx, bf16[128,1024]{1,0:T(8,128)(2,1)} %get-tuple-element.23.dqx, bf16[16,128,128]{2,1,0:T(8,128)(2,1)} %get-tuple-element.24.gk, ...), custom_call_target="tpu_custom_call" | custom-call | tf_op jit(solution)/shard_map/scatter/pallas_call | solution.py:456
  56.2 0.0 copy-start
  56.2 1.7 %copy.20 = bf16[64,2048]{1,0:T(8,128)(2,1)} copy(bf16[64,2048]{1,0:T(8,128)(2,1)} %get-tuple-element.30) | data formatting | bytes 524288
  58.0 0.0 copy-done
  58.0 0.0 copy-start.3
  58.0 0.7 %copy.21 = bf16[64,2048]{1,0:T(8,128)(2,1)} copy(bf16[64,2048]{1,0:T(8,128)(2,1)S(1)} %copy-done) | data formatting | bytes 524288
  58.7 0.1 copy-done.3
  58.7 0.0 copy-start.2
  58.7 0.6 %copy.22 = bf16[64,256]{1,0:T(8,128)(2,1)} copy(bf16[64,256]{1,0:T(8,128)(2,1)S(1)} %copy-done.3) | data formatting | bytes 65536
  59.3 0.2 copy-done.2
  59.5 0.6 %copy.23 = bf16[64,256]{1,0:T(8,128)(2,1)} copy(bf16[64,256]{1,0:T(8,128)(2,1)S(1)} %copy-done.2) | data formatting | bytes 65536
  (2 shorter events, 0.0 us)
Async XLA Ops:
  0.6 1.0 %copy-start.1 = (s32[4,16,8]{1,2,0:T(8,128)S(1)}, s32[4,16,8]{1,2,0:T(8,128)}, u32[]{:S(2)}) copy-start(s32[4,16,8]{1,2,0:T(8,128)} %param.9) | copy-start | bytes 6148
  56.2 1.7 %copy-start = (bf16[64,2048]{1,0:T(8,128)(2,1)S(1)}, bf16[64,2048]{1,0:T(8,128)(2,1)}, u32[]{:S(2)}) copy-start(bf16[64,2048]{1,0:T(8,128)(2,1)} %get-tuple-element.31) | copy-start | bytes 786436
  58.0 0.8 %copy-start.3 = (bf16[64,256]{1,0:T(8,128)(2,1)S(1)}, bf16[64,256]{1,0:T(8,128)(2,1)}, u32[]{:S(2)}) copy-start(bf16[64,256]{1,0:T(8,128)(2,1)} %get-tuple-element.32) | copy-start | bytes 98308
  58.7 0.8 %copy-start.2 = (bf16[64,256]{1,0:T(8,128)(2,1)S(1)}, bf16[64,256]{1,0:T(8,128)(2,1)}, u32[]{:S(2)}) copy-start(bf16[64,256]{1,0:T(8,128)(2,1)} %get-tuple-element.33) | copy-start | bytes 98308
